TPU v7x, 32 devices: a whole 2x2x4 slice. The times are simulated.
32 devices in a mesh: dp: 16 (over z, y, x), mp: 2 (over core).
Axes of the slice: x: 2, y: 2, z: 4, core: 2. Of those that a mesh axis runs over, the one named last changes fastest.
Arguments:
- tokens: bfloat16 [128, 288, 768], P('dp', None, 'mp'), may hold values from -6 to 6
- segment_ids: int32 [128, 288], P('dp'), may hold values from 0 to 3, never falling along the last dimension, each value on 1 to 144 neighbouring positions
- positions: int32 [128, 288], P('dp'), may hold values from 0 to 511
- query_vectors: float32 [16, 128], P('dp'), may hold values from -3 to 3
- doc_owner: int32 [16, 8], P('dp'), may hold values from 0 to 15, as said below
- doc_slot: int32 [16, 8], P('dp'), may hold values from 0 to 15
- doc_store: bfloat16 [256, 288, 768], P('dp', None, 'mp'), may hold values from -3 to 3
- pos_table: bfloat16 [512, 768], P(None, 'mp'), may hold values from -3 to 3
- w_query: bfloat16 [768, 768], P(None, 'mp'), may hold values from -0.21875 to 0.21875
- w_key: bfloat16 [768, 768], P(None, 'mp'), may hold values from -0.21875 to 0.21875
- w_value: bfloat16 [768, 768], P(None, 'mp'), may hold values from -0.21875 to 0.21875
- b_query: float32 [768], P('mp'), may hold values from -3 to 3
- b_value: float32 [768], P('mp'), may hold values from -3 to 3
- w_out: bfloat16 [768, 768], P('mp'), may hold values from -0.4375 to 0.4375
- b_out: float32 [768], P('mp'), may hold values from -2 to 2
- gain_attn: float32 [768], P('mp'), may hold values from 0.5 to 1.5
- shift_attn: float32 [768], P('mp'), may hold values from -2 to 2
- w_inner: bfloat16 [768, 3072], P(None, 'mp'), may hold values from -0.21875 to 0.21875
- b_inner: float32 [3072], P('mp'), may hold values from -3 to 3
- w_outer: bfloat16 [3072, 768], P('mp'), may hold values from -0.15625 to 0.15625
- b_outer: float32 [768], P('mp'), may hold values from -2 to 2
- gain_ffn: float32 [768], P('mp'), may hold values from 0.5 to 1.5
- shift_ffn: float32 [768], P('mp'), may hold values from -2 to 2
- w_cls: bfloat16 [768, 128], P('mp'), may hold values from -0.21875 to 0.21875
- cotangent: bfloat16 [16, 288, 768], P('dp', None, 'mp'), may hold values from -6 to 6
Outputs:
- mixed: bfloat16 [16, 288, 768], P('dp', None, 'mp')
- grad_tokens: bfloat16 [128, 288, 768], P('dp', None, 'mp')
- grad_query: float32 [16, 128], P('dp')
- grad_docs: float32 [256, 288, 768], P('dp', None, 'mp')
- grad_pos: float32 [512, 768], P('dp', 'mp')
- grad_wq: float32 [768, 768], P('dp', 'mp')
- grad_wk: float32 [768, 768], P('dp', 'mp')
- grad_wv: float32 [768, 768], P('dp', 'mp')
- grad_bq: float32 [768], P('mp')
- grad_bv: float32 [768], P('mp')
- grad_wo: float32 [768, 768], P('mp', 'dp')
- grad_bo: float32 [768], P('mp')
- grad_gain_attn: float32 [768], P('mp')
- grad_shift_attn: float32 [768], P('mp')
- grad_w_inner: float32 [768, 3072], P('dp', 'mp')
- grad_b_inner: float32 [3072], P('mp')
- grad_w_outer: float32 [3072, 768], P('mp', 'dp')
- grad_b_outer: float32 [768], P('mp')
- grad_gain_ffn: float32 [768], P('mp')
- grad_shift_ffn: float32 [768], P('mp')
- grad_w_cls: float32 [768, 128], P('mp', 'dp')
Inputs may be any that keep to these rules, and one draw needn't show every extreme that they name: `doc_owner`: the 8 owners in the row of dp index i are distinct and each is (i + o) mod 16 for an offset o with -6 <= o < 6. `segment_ids`: segment numbers never fall along a block; a segment holds at most 144 tokens.
All inputs are finite; a program needn't handle non-finite values.
Results may differ from a plain program's by a relative error of at most 0.019.
Values may be sent and summed in bfloat16 or wider, within the bound.
A program may use at most 256 MiB of HBM per device.

v0:
```python
import jax
import jax.numpy as jnp
from jax import lax
from jax.sharding import PartitionSpec as P

D = 768
HEAD_DIM = 64
PROJ = 128
MAXPOS = 512
TOPK = 8
SEQ = 288
REACH = 6


EPSILON = 1e-05
PRECISE = lax.Precision.HIGHEST
NEGATIVE = -1e30


def from_behind(value, axis, steps):
    count = lax.axis_size(axis)
    pairs = [(source, (source + steps) % count) for source in range(count)]
    return lax.ppermute(value, axis, pairs)


def widen(values):
    return lax.all_gather(values, "mp", axis=1, tiled=True)


def narrow(values):
    return lax.psum_scatter(values, "mp", scatter_dimension=1, tiled=True)


def route_blocks(rows, codes):
    moved_rows = []
    moved_codes = []
    for slot in range(2 * REACH):
        step = slot - REACH
        if step == 0:
            moved_rows.append(rows[slot])
            moved_codes.append(codes[slot])
        else:
            got_rows, got_codes = from_behind((rows[slot], codes[slot]), "dp", step)
            moved_rows.append(got_rows)
            moved_codes.append(got_codes)
    return (jnp.stack(moved_rows), jnp.stack(moved_codes))


def carry_blocks(rows, sign):
    moved = []
    for slot in range(2 * REACH):
        step = slot - REACH
        if step == 0:
            moved.append(rows[slot])
        else:
            moved.append(from_behind(rows[slot], "dp", sign * step))
    return jnp.stack(moved)


def pack_rows(match_low, rows):
    return jnp.einsum("wk,ksd->wsd", match_low, rows, preferred_element_type=jnp.float32).astype(
        jnp.bfloat16
    )


def unpack_rows(match_low, rows):
    return jnp.einsum("wk,wsd->ksd", match_low, rows, preferred_element_type=jnp.float32).astype(
        jnp.bfloat16
    )


def row_mean(values):
    return lax.psum(jnp.sum(values, axis=1), "mp") / D


def cross(left, right):
    return lax.dot_general(
        left, right, (((0,), (0,)), ((), ())), preferred_element_type=jnp.float32
    )


def against(left, right):
    return lax.dot_general(
        left, right, (((1,), (1,)), ((), ())), preferred_element_type=jnp.float32
    )


def gelu_exact(values):
    return jax.nn.gelu(values, approximate=False)


def norm_forward(hidden, gain, offset):
    average = row_mean(hidden)
    centered = hidden - average[:, None]
    spread = row_mean(centered * centered)
    inverse = lax.rsqrt(spread + EPSILON)
    normed = centered * inverse[:, None]
    return (normed * gain + offset, normed, inverse)


def norm_backward(upstream, normed, inverse, gain):
    scaled = upstream * gain
    first_sum, second_sum = lax.psum(
        (jnp.sum(scaled, axis=1), jnp.sum(scaled * normed, axis=1)), "mp"
    )
    inside = scaled - first_sum[:, None] / D - normed * (second_sum[:, None] / D)
    return (
        inverse[:, None] * inside,
        jnp.sum(upstream * normed, axis=0),
        jnp.sum(upstream, axis=0),
    )


def masked_scores(queries, key_heads, same_seg):
    scores = jnp.einsum(
        "bqhd,bkhd->bhqk", queries, key_heads, preferred_element_type=jnp.float32
    ) * HEAD_DIM ** (-0.5)
    return jnp.where(same_seg, scores, NEGATIVE)


def attend_group(pieces):
    queries, key_heads, values, same_seg = pieces
    scores = masked_scores(queries, key_heads, same_seg)
    highest = jnp.max(scores, axis=-1, keepdims=True)
    log_total = highest + jnp.log(jnp.sum(jnp.exp(scores - highest), axis=-1, keepdims=True))
    weights_low = jnp.exp(scores - log_total).astype(jnp.bfloat16)
    context = jnp.einsum("bhqk,bkhd->bqhd", weights_low, values, preferred_element_type=jnp.float32)
    return (context, log_total)


def attend_back(pieces):
    queries, key_heads, values, same_seg, log_total, dcontext = pieces
    weights = jnp.exp(masked_scores(queries, key_heads, same_seg) - log_total)
    dvalues = jnp.einsum(
        "bhqk,bqhd->bkhd",
        weights.astype(jnp.bfloat16),
        dcontext,
        preferred_element_type=jnp.float32,
    )
    dweights = jnp.einsum("bqhd,bkhd->bhqk", dcontext, values, preferred_element_type=jnp.float32)
    dscores_low = (
        weights * (dweights - jnp.sum(weights * dweights, axis=-1, keepdims=True))
    ).astype(jnp.bfloat16)
    factor = HEAD_DIM ** (-0.5)
    dqueries = (
        jnp.einsum("bhqk,bkhd->bqhd", dscores_low, key_heads, preferred_element_type=jnp.float32)
        * factor
    )
    dkey_heads = (
        jnp.einsum("bhqk,bqhd->bkhd", dscores_low, queries, preferred_element_type=jnp.float32)
        * factor
    )
    return (dqueries, dkey_heads, dvalues)


def embed_half(tokens_here, doc_part, places, pos_table):
    width_here = pos_table.shape[1]
    one_hot = (places.reshape(-1)[:, None] == jnp.arange(MAXPOS, dtype=jnp.int32)[None, :]).astype(
        jnp.bfloat16
    )
    from_pos = jnp.dot(one_hot, pos_table, preferred_element_type=jnp.float32)
    summed = tokens_here.reshape(-1, width_here).astype(jnp.float32) + from_pos
    summed = summed + doc_part.reshape(-1, width_here).astype(jnp.float32)
    return (summed, one_hot)


def reader_forward(embedded, seg_keys, params):
    (
        w_query,
        w_key,
        w_value,
        b_query,
        b_value,
        w_out,
        b_out,
        gain_attn,
        shift_attn,
        w_inner,
        b_inner,
        w_outer,
        b_outer,
        gain_ffn,
        shift_ffn,
    ) = params
    blocks = seg_keys.shape[0]
    width_here = w_query.shape[1]
    embedded_full = widen(embedded.astype(jnp.bfloat16))
    queries = (
        jnp.dot(embedded_full, w_query, preferred_element_type=jnp.float32) + b_query
    ).astype(jnp.bfloat16)
    key_heads = jnp.dot(embedded_full, w_key, preferred_element_type=jnp.float32).astype(
        jnp.bfloat16
    )
    values = (jnp.dot(embedded_full, w_value, preferred_element_type=jnp.float32) + b_value).astype(
        jnp.bfloat16
    )
    head_shape = (blocks // 2, 2, SEQ, width_here // HEAD_DIM, HEAD_DIM)
    same_seg = (seg_keys[:, None, :, None] == seg_keys[:, None, None, :]).reshape(
        blocks // 2, 2, 1, SEQ, SEQ
    )
    context, log_total = lax.map(
        attend_group,
        (
            queries.reshape(head_shape),
            key_heads.reshape(head_shape),
            values.reshape(head_shape),
            same_seg,
        ),
    )
    context_low = context.reshape(blocks * SEQ, width_here).astype(jnp.bfloat16)
    attended = narrow(jnp.dot(context_low, w_out, preferred_element_type=jnp.float32))
    middle, normed_mid, inverse_mid = norm_forward(
        embedded + attended + b_out, gain_attn, shift_attn
    )
    middle_full = widen(middle.astype(jnp.bfloat16))
    inner_pre = jnp.dot(middle_full, w_inner, preferred_element_type=jnp.float32) + b_inner
    active_low = gelu_exact(inner_pre).astype(jnp.bfloat16)
    outer_sum = narrow(jnp.dot(active_low, w_outer, preferred_element_type=jnp.float32))
    result, normed_out, inverse_out = norm_forward(
        middle + outer_sum + b_outer, gain_ffn, shift_ffn
    )
    stored = (
        embedded_full,
        queries,
        key_heads,
        values,
        same_seg,
        log_total,
        context_low,
        normed_mid,
        inverse_mid,
        middle_full,
        inner_pre,
        active_low,
        normed_out,
        inverse_out,
    )
    return (result.astype(jnp.bfloat16), stored)


def reader_backward(upstream, stored, params):
    (
        w_query,
        w_key,
        w_value,
        b_query,
        b_value,
        w_out,
        b_out,
        gain_attn,
        shift_attn,
        w_inner,
        b_inner,
        w_outer,
        b_outer,
        gain_ffn,
        shift_ffn,
    ) = params
    (
        embedded_full,
        queries,
        key_heads,
        values,
        same_seg,
        log_total,
        context_low,
        normed_mid,
        inverse_mid,
        middle_full,
        inner_pre,
        active_low,
        normed_out,
        inverse_out,
    ) = stored
    blocks = same_seg.shape[0] * 2
    width_here = w_query.shape[1]
    head_shape = (blocks // 2, 2, SEQ, width_here // HEAD_DIM, HEAD_DIM)
    dsum_out, dgain_ffn, dshift_ffn = norm_backward(upstream, normed_out, inverse_out, gain_ffn)
    douter_full = widen(dsum_out.astype(jnp.bfloat16))
    dw_outer = cross(active_low, douter_full)
    dactive = against(douter_full, w_outer)
    dinner = jax.vjp(gelu_exact, inner_pre)[1](dactive)[0]
    dinner_low = dinner.astype(jnp.bfloat16)
    dw_inner = cross(middle_full, dinner_low)
    dmiddle = dsum_out + narrow(against(dinner_low, w_inner))
    dsum_mid, dgain_attn, dshift_attn = norm_backward(dmiddle, normed_mid, inverse_mid, gain_attn)
    dattn_full = widen(dsum_mid.astype(jnp.bfloat16))
    dw_out = cross(context_low, dattn_full)
    dcontext = against(dattn_full, w_out).astype(jnp.bfloat16)
    dqueries, dkey_heads, dvalues = lax.map(
        attend_back,
        (
            queries.reshape(head_shape),
            key_heads.reshape(head_shape),
            values.reshape(head_shape),
            same_seg,
            log_total,
            dcontext.reshape(head_shape),
        ),
    )
    dquery_low = dqueries.reshape(blocks * SEQ, width_here).astype(jnp.bfloat16)
    dkey_low = dkey_heads.reshape(blocks * SEQ, width_here).astype(jnp.bfloat16)
    dvalue_low = dvalues.reshape(blocks * SEQ, width_here).astype(jnp.bfloat16)
    dw_query = cross(embedded_full, dquery_low)
    dw_key = cross(embedded_full, dkey_low)
    dw_value = cross(embedded_full, dvalue_low)
    through = against(dquery_low, w_query) + against(dkey_low, w_key) + against(dvalue_low, w_value)
    dstart = dsum_mid + narrow(through)
    matrices = (dw_query, dw_key, dw_value, dw_out, dw_inner, dw_outer)
    vectors = (
        jnp.sum(dquery_low.astype(jnp.float32), axis=0),
        jnp.sum(dvalue_low.astype(jnp.float32), axis=0),
        jnp.sum(dsum_mid, axis=0),
        dgain_attn,
        dshift_attn,
        jnp.sum(dinner, axis=0),
        jnp.sum(dsum_out, axis=0),
        dgain_ffn,
        dshift_ffn,
    )
    return (dstart.astype(jnp.bfloat16), matrices, vectors)


def body(
    tokens,
    segment_ids,
    positions,
    query_vectors,
    doc_owner,
    doc_slot,
    doc_store,
    pos_table,
    w_query,
    w_key,
    w_value,
    b_query,
    b_value,
    w_out,
    b_out,
    gain_attn,
    shift_attn,
    w_inner,
    b_inner,
    w_outer,
    b_outer,
    gain_ffn,
    shift_ffn,
    w_cls,
    cotangent,
):
    params = (
        w_query,
        w_key,
        w_value,
        b_query,
        b_value,
        w_out,
        b_out,
        gain_attn,
        shift_attn,
        w_inner,
        b_inner,
        w_outer,
        b_outer,
        gain_ffn,
        shift_ffn,
    )
    devices = lax.axis_size("dp")
    my_index = lax.axis_index("dp")
    row_count, seq_len, width_here = tokens.shape
    owners = doc_owner[0]
    slot_ids = doc_slot[0]
    doc_count = doc_store.shape[0]
    offsets = (owners - my_index + REACH) % devices - REACH
    match_int = (offsets[None, :] == jnp.arange(-REACH, REACH, dtype=jnp.int32)[:, None]).astype(
        jnp.int32
    )
    match_low = match_int.astype(jnp.bfloat16)
    token_codes = 1 + positions + MAXPOS * (segment_ids + seq_len * slot_ids[:, None])
    sent_codes = jnp.sum(match_int[:, :, None] * token_codes[None, :, :], axis=1)
    arrived, arrived_codes = route_blocks(pack_rows(match_low, tokens), sent_codes)
    local_codes = arrived_codes - 1
    seg_keys = local_codes // MAXPOS
    doc_target = jnp.where(local_codes[:, 0] >= 0, seg_keys[:, 0] // seq_len, doc_count)
    doc_part = doc_store.at[doc_target].get(mode="fill", fill_value=0)
    embedded, one_hot = embed_half(arrived, doc_part, local_codes % MAXPOS, pos_table)
    result, stored = reader_forward(embedded, seg_keys, params)
    back_rows = carry_blocks(result.reshape(2 * REACH, seq_len, width_here), -1)
    returned_mine = unpack_rows(match_low, back_rows)
    grouped = returned_mine.reshape(row_count // TOPK, TOPK, seq_len, width_here)
    summary_part = jnp.dot(returned_mine[:, 0, :], w_cls, preferred_element_type=jnp.float32)
    summary = lax.psum(summary_part, "mp")
    summary = summary.reshape(row_count // TOPK, TOPK, -1)
    inv_root = PROJ ** (-0.5)
    shares = jax.nn.softmax(
        jnp.sum(summary * query_vectors[:, None, :], axis=-1) * inv_root, axis=-1
    )
    mixed = jnp.einsum("qk,qksd->qsd", shares, grouped.astype(jnp.float32), precision=PRECISE)
    product = lax.psum(
        jnp.einsum("qsd,qksd->qk", cotangent, grouped, preferred_element_type=jnp.float32), "mp"
    )
    dlogits = shares * (product - jnp.sum(shares * product, axis=-1, keepdims=True))
    grad_query = jnp.sum(dlogits[..., None] * summary, axis=1) * inv_root
    dsummary = (dlogits[..., None] * query_vectors[:, None, :] * inv_root).reshape(row_count, -1)
    heads_row = returned_mine[:, 0, :].astype(jnp.float32)
    dw_cls = jnp.dot(heads_row.T, dsummary, precision=PRECISE)
    dreturn = (shares[..., None, None] * cotangent.astype(jnp.float32)[:, None]).reshape(
        row_count, seq_len, width_here
    )
    dreturn = dreturn.at[:, 0, :].add(
        jnp.dot(dsummary, w_cls.astype(jnp.float32).T, precision=PRECISE)
    )
    dreturn_low = dreturn.astype(jnp.bfloat16)
    grad_shape = (doc_count, seq_len, width_here)
    upstream = carry_blocks(pack_rows(match_low, dreturn_low), 1)
    dstart, matrices, vectors = reader_backward(
        upstream.reshape(-1, width_here).astype(jnp.float32), stored, params
    )
    dstart_rows = dstart.reshape(2 * REACH, seq_len, width_here)
    grad_docs = (
        jnp.zeros(grad_shape, jnp.float32)
        .at[doc_target]
        .add(dstart_rows.astype(jnp.float32), mode="drop")
    )
    grad_tokens = unpack_rows(match_low, carry_blocks(dstart_rows, -1))
    grad_pos_part = cross(one_hot, dstart)
    dw_query, dw_key, dw_value, dw_out, dw_inner, dw_outer = matrices
    (
        dbias_query,
        dbias_value,
        dbias_out,
        dgain_attn,
        dshift_attn,
        dbias_inner,
        dbias_outer,
        dgain_ffn,
        dshift_ffn,
    ) = vectors
    summed_mats = (
        lax.psum_scatter(dw_query, "dp", scatter_dimension=0, tiled=True),
        lax.psum_scatter(dw_key, "dp", scatter_dimension=0, tiled=True),
        lax.psum_scatter(dw_value, "dp", scatter_dimension=0, tiled=True),
        lax.psum_scatter(dw_out, "dp", scatter_dimension=1, tiled=True),
        lax.psum_scatter(dw_inner, "dp", scatter_dimension=0, tiled=True),
        lax.psum_scatter(dw_outer, "dp", scatter_dimension=1, tiled=True),
        lax.psum_scatter(dw_cls, "dp", scatter_dimension=1, tiled=True),
        lax.psum_scatter(grad_pos_part, "dp", scatter_dimension=0, tiled=True),
    )
    summed_vecs = lax.psum(
        (
            dbias_query,
            dbias_value,
            dbias_out,
            dgain_attn,
            dshift_attn,
            dbias_inner,
            dbias_outer,
            dgain_ffn,
            dshift_ffn,
        ),
        "dp",
    )
    return (
        mixed.astype(jnp.bfloat16),
        grad_tokens,
        grad_query,
        grad_docs,
        summed_mats[7],
        summed_mats[0],
        summed_mats[1],
        summed_mats[2],
        summed_vecs[0],
        summed_vecs[1],
        summed_mats[3],
        summed_vecs[2],
        summed_vecs[3],
        summed_vecs[4],
        summed_mats[4],
        summed_vecs[5],
        summed_mats[5],
        summed_vecs[6],
        summed_vecs[7],
        summed_vecs[8],
        summed_mats[6],
    )


def solution(mesh):
    in_specs = (
        P("dp", None, "mp"),
        P("dp", None),
        P("dp", None),
        P("dp", None),
        P("dp", None),
        P("dp", None),
        P("dp", None, "mp"),
        P(None, "mp"),
        P(None, "mp"),
        P(None, "mp"),
        P(None, "mp"),
        P("mp"),
        P("mp"),
        P("mp", None),
        P("mp"),
        P("mp"),
        P("mp"),
        P(None, "mp"),
        P("mp"),
        P("mp", None),
        P("mp"),
        P("mp"),
        P("mp"),
        P("mp", None),
        P("dp", None, "mp"),
    )
    out_specs = (
        P("dp", None, "mp"),
        P("dp", None, "mp"),
        P("dp", None),
        P("dp", None, "mp"),
        P("dp", "mp"),
        P("dp", "mp"),
        P("dp", "mp"),
        P("dp", "mp"),
        P("mp"),
        P("mp"),
        P("mp", "dp"),
        P("mp"),
        P("mp"),
        P("mp"),
        P("dp", "mp"),
        P("mp"),
        P("mp", "dp"),
        P("mp"),
        P("mp"),
        P("mp"),
        P("mp", "dp"),
    )
    return jax.shard_map(body, mesh=mesh, in_specs=in_specs, out_specs=out_specs, check_vma=False)
```

profile of v0, /device:TPU:0, one launch (start us, length us, event | category | flops | bytes accessed | tf_op | source)
XLA Modules:
  0.0 1961.7 jit_solution(915944622762086214)
XLA Ops:
  95.3 20.0 %collective-permute-done.10 = bf16[288,384]{1,0:T(8,128)(2,1)S(1)} collective-permute-done((bf16[288,384]{1,0:T(8,128)(2,1)S(1)}, bf16[288,384]{1,0:T(8,128)(2,1)S(1)}, u32[]{:S(2)}, u32[]{:S(2)}) %collective-permute-start.10) | collective-permute-done | bytes 221216 | tf_op jit(solution)/shard_map/ppermute | solution.py:23
  150.0 9.1 copy.537
  175.0 9.2 copy.538
  211.5 46.1 %while.27 = (s32[]{:T(128)}, bf16[6,2,288,6,64]{2,4,3,1,0:T(8,128)(2,1)}, f32[6,2,6,288,1]{3,2,1,4,0:T(8,128)}, bf16[6,2,288,6,64]{2,4,3,1,0:T(8,128)(2,1)}, pre...) while((s32[]{:T(128)}, ...), condition=%wide.region_4.5_spmd, body=%wide.region_1.4_spmd.sunk | while | flops 265749120 | bytes 15846489 | solution.py:201
  276.9 19.1 reduce-scatter.12.cloned.1.call-done
  320.0 16.5 all-gather.7.cloned.1.call-done
  336.5 55.7 %multiply_convert_fusion.1 = (bf16[3456,1536]{1,0:T(8,128)(2,1)S(1)}, f32[3456,1536]{1,0:T(8,128)}, f32[3456,1536]{1,0:T(8,128)}) fusion(f32[1536]{0:T(1024)S(1)} %copy-done.81, bf16[3456,768]{1,0:T(8,128)(2,1)} %all-gather.7.cloned.1.call-done, bf16[768,1536]{1,0:T(8,128)(2,1)} %param.48), kind=kOutput, calls=%fused_computation.72 | convolution fusion | flops 8504082432 | bytes 60758016 | tf_op jit(solution)/shard_map/dot_general | solution.py:216
  396.3 11.5 fusion.138
  407.9 20.4 %reduce-scatter.14.cloned.1.call-done = f32[3456,384]{1,0:T(8,128)} async-done(((f32[3456,768]{1,0:T(8,128)}), f32[3456,384]{1,0:T(8,128)}) %reduce-scatter.14.cloned.1.call-update) | async-done | bytes 5308432 | tf_op jit(solution)/shard_map/reduce_scatter | solution.py:31
  460.1 24.5 %collective-permute-done.22 = bf16[288,384]{1,0:T(8,128)(2,1)S(1)} collective-permute-done((bf16[288,384]{1,0:T(8,128)(2,1)S(1)}, bf16[288,384]{1,0:T(8,128)(2,1)S(1)}, u32[]{:S(2)}, u32[]{:S(2)}) %collective-permute-start.22) | collective-permute-done | bytes 221216 | tf_op jit(solution)/shard_map/ppermute | solution.py:23
  547.6 29.0 %collective-permute-start.38 = (bf16[288,384]{1,0:T(8,128)(2,1)S(1)}, bf16[288,384]{1,0:T(8,128)(2,1)S(1)}, u32[]{:S(2)}, u32[]{:S(2)}) collective-permute-start(bf16[288,384]{1,0:T(8,128)(2,1)S(1)} %bitcast.401), channel_id=1, source_target_pairs={{0,30},{2,0},{4,2},{6,4},{8,6},{10,8},{12,10},{14,12},{16,14},{18,... | collective-permute-start | bytes 663560 | tf_op jit(solution)/shard_map/ppermute | solution.py:23
  594.9 15.6 collective-permute-done.43
  611.6 17.3 stack.305
  652.3 11.2 all-gather.9.cloned.1.call-done
  663.5 26.8 %fusion.136 = (f32[1536]{0:T(1024)}, bf16[3456,1536]{1,0:T(8,128)(2,1)}) fusion(f32[3456,1536]{1,0:T(8,128)} %get-tuple-element.666, bf16[3456,768]{1,0:T(8,128)(2,1)} %all-gather.9.cloned.1.call-done, bf16[1536,768]{1,0:T(8,128)(2,1)S(1)} %copy-done.79, f32[3456,1536]{1,0:T(8,128)} %get-tuple-element.726, f32[1536]{0:T(1024)S(1)} %copy-done.82), kind=kOutput, calls=%fused_computation.331 | convolution fusion | flops 8238660096 | bytes 60764160 | tf_op jit(solution)/shard_map/dot_general | solution.py:83
  690.3 14.3 fusion.73
  704.7 20.4 %reduce-scatter.16.cloned.1.call-done = f32[3456,384]{1,0:T(8,128)} async-done(((f32[3456,768]{1,0:T(8,128)}), f32[3456,384]{1,0:T(8,128)}) %reduce-scatter.16.cloned.1.call-update) | async-done | bytes 5308432 | tf_op jit(solution)/shard_map/reduce_scatter | solution.py:31
  725.2 10.1 multiply_reduce_fusion.2
  752.0 14.4 all-gather.11.cloned.1.call-done
  778.4 9.1 copy.558
  794.6 105.1 %while.28 = (s32[]{:T(128)}, bf16[6,2,288,6,64]{2,4,3,1,0:T(8,128)(2,1)}, bf16[6,2,288,6,64]{2,4,3,1,0:T(8,128)(2,1)}, bf16[6,2,288,6,64]{2,4,3,1,0:T(8,128)(2,1...) while((s32[]{:T(128)}, ...), condition=%wide.region_32.33_spmd, body=%wide.region_30.32_spmd.sunk | while | flops 652378752 | bytes 38458996 | solution.py:290
  943.1 15.1 add_add_fusion
  958.3 14.8 fusion.145
  973.2 16.2 fusion.71
  1029.1 78.4 %all-reduce.1 = (f32[384]{0:T(512)}, f32[384]{0:T(512)}, f32[384]{0:T(512)}, f32[384]{0:T(512)}, f32[384]{0:T(512)}, /*index=5*/f32[1536]{0:T(1024)}, f32[384]{0:T(512)}, f32[384]{0:T(512)}, f32[384]{0:T(512)}) all-reduce(f32[384]{0:T(512)S(1)} %reduce_sum.237, f32[384]{0:T(512)S(1)} %reduce_sum.239, ...), channel_id=1, replica_groups=mesh['dp'=16,'mp'=2] {'dp'}, use_global_device_ids=true, to_apply=%region_41.42 | all-reduce | flops 4608 | bytes 36864 | tf_op jit(solution)/shard_map/psum | solution.py:449
  1127.0 12.2 scatter_fusion
  1170.9 142.6 %reduce-scatter.30.cloned.1.call-done = f32[48,1536]{1,0:T(8,128)} async-done(((f32[768,1536]{1,0:T(8,128)}), f32[48,1536]{1,0:T(8,128)}) %reduce-scatter.30.cloned.1.call-update) | async-done | bytes 294928 | tf_op jit(solution)/shard_map/reduce_scatter | solution.py:444
  1313.5 128.6 %reduce-scatter.28.cloned.1.call-done = f32[384,48]{0,1:T(8,128)} async-done(((f32[384,768]{0,1:T(8,128)}), f32[384,48]{0,1:T(8,128)}) %reduce-scatter.28.cloned.1.call-update) | async-done | bytes 73744 | tf_op jit(solution)/shard_map/reduce_scatter | solution.py:443
  1442.1 128.7 %reduce-scatter.22.cloned.1.call-done = f32[48,384]{1,0:T(8,128)} async-done(((f32[768,384]{1,0:T(8,128)}), f32[48,384]{1,0:T(8,128)}) %reduce-scatter.22.cloned.1.call-update) | async-done | bytes 73744 | tf_op jit(solution)/shard_map/reduce_scatter | solution.py:440
  1570.8 128.5 %reduce-scatter.24.cloned.1.call-done = f32[48,384]{1,0:T(8,128)} async-done(((f32[768,384]{1,0:T(8,128)}), f32[48,384]{1,0:T(8,128)}) %reduce-scatter.24.cloned.1.call-update) | async-done | bytes 73744 | tf_op jit(solution)/shard_map/reduce_scatter | solution.py:441
  1699.3 128.5 %reduce-scatter.26.cloned.1.call-done = f32[48,384]{1,0:T(8,128)} async-done(((f32[768,384]{1,0:T(8,128)}), f32[48,384]{1,0:T(8,128)}) %reduce-scatter.26.cloned.1.call-update) | async-done | bytes 73744 | tf_op jit(solution)/shard_map/reduce_scatter | solution.py:442
  1827.8 127.2 %reduce-scatter.20.cloned.1.call-done = f32[32,384]{1,0:T(8,128)} async-done(((f32[512,384]{1,0:T(8,128)}), f32[32,384]{1,0:T(8,128)}) %reduce-scatter.20.cloned.1.call-update) | async-done | bytes 49168 | tf_op jit(solution)/shard_map/reduce_scatter | solution.py:447
  (608 shorter events, 669.0 us)
Async XLA Ops:
  7.2 126.9 %all-gather.5.cloned.1.call-start = ((), (), s32[]{:S(2)}) async-start(), calls=%async_computation.11 | async-start | bytes 7962624 | tf_op jit(solution)/shard_map/all_gather | solution.py:27
  39.8 31.0 %collective-permute-start = (bf16[288,384]{1,0:T(8,128)(2,1)}, bf16[288,384]{1,0:T(8,128)(2,1)}, u32[]{:S(2)}, u32[]{:S(2)}) collective-permute-start(bf16[288,384]{1,0:T(8,128)(2,1)} %get-tuple-element.720), channel_id=1, source_target_pairs={{0,20},{2,22},{4,24},{6,26},{8,28},{10,30},{12,0},{14,2},{16,4},{1... | collective-permute-start | bytes 663560 | tf_op jit(solution)/shard_map/ppermute | solution.py:23
  45.4 31.5 %collective-permute-start.1 = (bf16[288,384]{1,0:T(8,128)(2,1)}, bf16[288,384]{1,0:T(8,128)(2,1)}, u32[]{:S(2)}, u32[]{:S(2)}) collective-permute-start(bf16[288,384]{1,0:T(8,128)(2,1)} %get-tuple-element.719), channel_id=1, source_target_pairs={{0,22},{2,24},{4,26},{6,28},{8,30},{10,0},{12,2},{14,4},{16,6},{18... | collective-permute-start | bytes 663560 | tf_op jit(solution)/shard_map/ppermute | solution.py:23
  121.5 174.4 %reduce-scatter.12.cloned.1.call-start = ((), (), s32[]{:S(2)}) async-start(), calls=%async_computation.12 | async-start | bytes 15925248 | tf_op jit(solution)/shard_map/reduce_scatter | solution.py:31
  276.8 59.7 %all-gather.7.cloned.1.call-start = ((), (), s32[]{:S(2)}) async-start(), calls=%async_computation.13 | async-start | bytes 7962624 | tf_op jit(solution)/shard_map/all_gather | solution.py:27
  320.0 108.3 %reduce-scatter.14.cloned.1.call-start = ((), (), s32[]{:S(2)}) async-start(), calls=%async_computation.14 | async-start | bytes 15925248 | tf_op jit(solution)/shard_map/reduce_scatter | solution.py:31
  407.8 255.7 %all-gather.9.cloned.1.call-start = ((), (), s32[]{:S(2)}) async-start(), calls=%async_computation.15 | async-start | bytes 7962624 | tf_op jit(solution)/shard_map/all_gather | solution.py:27
  451.4 33.2 %collective-permute-start.22 = (bf16[288,384]{1,0:T(8,128)(2,1)S(1)}, bf16[288,384]{1,0:T(8,128)(2,1)S(1)}, u32[]{:S(2)}, u32[]{:S(2)}) collective-permute-start(bf16[288,384]{1,0:T(8,128)(2,1)S(1)} %get-tuple-element.708), channel_id=1, source_target_pairs={{0,12},{2,14},{4,16},{6,18},{8,20},{10,22},{12,24},{14,26},{16,28}... | collective-permute-start | bytes 663560 | tf_op jit(solution)/shard_map/ppermute | solution.py:23
  454.2 40.1 %collective-permute-start.23 = (bf16[288,384]{1,0:T(8,128)(2,1)S(1)}, bf16[288,384]{1,0:T(8,128)(2,1)S(1)}, u32[]{:S(2)}, u32[]{:S(2)}) collective-permute-start(bf16[288,384]{1,0:T(8,128)(2,1)S(1)} %get-tuple-element.707), channel_id=1, source_target_pairs={{0,10},{2,12},{4,14},{6,16},{8,18},{10,20},{12,22},{14,24},{16,26}... | collective-permute-start | bytes 663560 | tf_op jit(solution)/shard_map/ppermute | solution.py:23
  456.6 37.7 %collective-permute-start.24 = (bf16[288,384]{1,0:T(8,128)(2,1)S(1)}, bf16[288,384]{1,0:T(8,128)(2,1)S(1)}, u32[]{:S(2)}, u32[]{:S(2)}) collective-permute-start(bf16[288,384]{1,0:T(8,128)(2,1)S(1)} %get-tuple-element.706), channel_id=1, source_target_pairs={{0,8},{2,10},{4,12},{6,14},{8,16},{10,18},{12,20},{14,22},{16,24},... | collective-permute-start | bytes 663560 | tf_op jit(solution)/shard_map/ppermute | solution.py:23
  458.1 36.3 %collective-permute-start.25 = (bf16[288,384]{1,0:T(8,128)(2,1)S(1)}, bf16[288,384]{1,0:T(8,128)(2,1)S(1)}, u32[]{:S(2)}, u32[]{:S(2)}) collective-permute-start(bf16[288,384]{1,0:T(8,128)(2,1)S(1)} %get-tuple-element.705), channel_id=1, source_target_pairs={{0,6},{2,8},{4,10},{6,12},{8,14},{10,16},{12,18},{14,20},{16,22},{... | collective-permute-start | bytes 663560 | tf_op jit(solution)/shard_map/ppermute | solution.py:23
  459.5 35.0 %collective-permute-start.26 = (bf16[288,384]{1,0:T(8,128)(2,1)S(1)}, bf16[288,384]{1,0:T(8,128)(2,1)S(1)}, u32[]{:S(2)}, u32[]{:S(2)}) collective-permute-start(bf16[288,384]{1,0:T(8,128)(2,1)S(1)} %get-tuple-element.704), channel_id=1, source_target_pairs={{0,4},{2,6},{4,8},{6,10},{8,12},{10,14},{12,16},{14,18},{16,20},{1... | collective-permute-start | bytes 663560 | tf_op jit(solution)/shard_map/ppermute | solution.py:23
  532.1 44.7 %collective-permute-start.34 = (bf16[288,384]{1,0:T(8,128)(2,1)S(1)}, bf16[288,384]{1,0:T(8,128)(2,1)S(1)}, u32[]{:S(2)}, u32[]{:S(2)}) collective-permute-start(bf16[288,384]{1,0:T(8,128)(2,1)S(1)} %bitcast.408), channel_id=1, source_target_pairs={{0,22},{2,24},{4,26},{6,28},{8,30},{10,0},{12,2},{14,4},{16,6},{18... | collective-permute-start | bytes 663560 | tf_op jit(solution)/shard_map/ppermute | solution.py:23
  537.4 39.5 %collective-permute-start.35 = (bf16[288,384]{1,0:T(8,128)(2,1)S(1)}, bf16[288,384]{1,0:T(8,128)(2,1)S(1)}, u32[]{:S(2)}, u32[]{:S(2)}) collective-permute-start(bf16[288,384]{1,0:T(8,128)(2,1)S(1)} %bitcast.406), channel_id=1, source_target_pairs={{0,24},{2,26},{4,28},{6,30},{8,0},{10,2},{12,4},{14,6},{16,8},{18,... | collective-permute-start | bytes 663560 | tf_op jit(solution)/shard_map/ppermute | solution.py:23
  539.4 37.6 %collective-permute-start.36 = (bf16[288,384]{1,0:T(8,128)(2,1)S(1)}, bf16[288,384]{1,0:T(8,128)(2,1)S(1)}, u32[]{:S(2)}, u32[]{:S(2)}) collective-permute-start(bf16[288,384]{1,0:T(8,128)(2,1)S(1)} %bitcast.404), channel_id=1, source_target_pairs={{0,26},{2,28},{4,30},{6,0},{8,2},{10,4},{12,6},{14,8},{16,10},{18,... | collective-permute-start | bytes 663560 | tf_op jit(solution)/shard_map/ppermute | solution.py:23
  544.5 32.6 %collective-permute-start.37 = (bf16[288,384]{1,0:T(8,128)(2,1)S(1)}, bf16[288,384]{1,0:T(8,128)(2,1)S(1)}, u32[]{:S(2)}, u32[]{:S(2)}) collective-permute-start(bf16[288,384]{1,0:T(8,128)(2,1)S(1)} %bitcast.402), channel_id=1, source_target_pairs={{0,28},{2,30},{4,0},{6,2},{8,4},{10,6},{12,8},{14,10},{16,12},{18,... | collective-permute-start | bytes 663560 | tf_op jit(solution)/shard_map/ppermute | solution.py:23
  547.6 34.9 %collective-permute-start.38 = (bf16[288,384]{1,0:T(8,128)(2,1)S(1)}, bf16[288,384]{1,0:T(8,128)(2,1)S(1)}, u32[]{:S(2)}, u32[]{:S(2)}) collective-permute-start(bf16[288,384]{1,0:T(8,128)(2,1)S(1)} %bitcast.401), channel_id=1, source_target_pairs={{0,30},{2,0},{4,2},{6,4},{8,6},{10,8},{12,10},{14,12},{16,14},{18,... | collective-permute-start | bytes 663560 | tf_op jit(solution)/shard_map/ppermute | solution.py:23
  652.1 73.1 %reduce-scatter.16.cloned.1.call-start = ((), (), s32[]{:S(2)}) async-start(), calls=%async_computation.16 | async-start | bytes 15925248 | tf_op jit(solution)/shard_map/reduce_scatter | solution.py:31
  704.7 61.7 %all-gather.11.cloned.1.call-start = ((), (), s32[]{:S(2)}) async-start(), calls=%async_computation.17 | async-start | bytes 7962624 | tf_op jit(solution)/shard_map/all_gather | solution.py:27
  749.9 266.6 %all-reduce.7.cloned.1.call-start = ((), (), s32[]{:S(2)}) async-start(), calls=%async_computation.26 | async-start | bytes 393216
  751.7 355.7 %reduce-scatter.18.cloned.1.call-start = ((), (), s32[]{:S(2)}) async-start(), calls=%async_computation.18 | async-start | bytes 15925248 | tf_op jit(solution)/shard_map/reduce_scatter | solution.py:31
  958.3 212.6 %reduce-scatter.32.cloned.1.call-start = ((), (), s32[]{:S(2)}) async-start(), calls=%async_computation.25 | async-start | bytes 5013504 | tf_op jit(solution)/shard_map/reduce_scatter | solution.py:445
  973.2 340.3 %reduce-scatter.30.cloned.1.call-start = ((), (), s32[]{:S(2)}) async-start(), calls=%async_computation.24 | async-start | bytes 5013504 | tf_op jit(solution)/shard_map/reduce_scatter | solution.py:444
  989.4 452.7 %reduce-scatter.28.cloned.1.call-start = ((), (), s32[]{:S(2)}) async-start(), calls=%async_computation.23 | async-start | bytes 1253376 | tf_op jit(solution)/shard_map/reduce_scatter | solution.py:443
  996.1 574.7 %reduce-scatter.22.cloned.1.call-start = ((), (), s32[]{:S(2)}) async-start(), calls=%async_computation.20 | async-start | bytes 1253376 | tf_op jit(solution)/shard_map/reduce_scatter | solution.py:440
  1004.2 695.1 %reduce-scatter.24.cloned.1.call-start = ((), (), s32[]{:S(2)}) async-start(), calls=%async_computation.21 | async-start | bytes 1253376 | tf_op jit(solution)/shard_map/reduce_scatter | solution.py:441
  1010.8 817.0 %reduce-scatter.26.cloned.1.call-start = ((), (), s32[]{:S(2)}) async-start(), calls=%async_computation.22 | async-start | bytes 1253376 | tf_op jit(solution)/shard_map/reduce_scatter | solution.py:442
  1025.6 929.3 %reduce-scatter.20.cloned.1.call-start = ((), (), s32[]{:S(2)}) async-start(), calls=%async_computation.19 | async-start | bytes 835584 | tf_op jit(solution)/shard_map/reduce_scatter | solution.py:447
  1113.5 32.3 %collective-permute-start.45 = (bf16[288,384]{1,0:T(8,128)(2,1)}, bf16[288,384]{1,0:T(8,128)(2,1)}, u32[]{:S(2)}, u32[]{:S(2)}) collective-permute-start(bf16[288,384]{1,0:T(8,128)(2,1)} %get-tuple-element.696), channel_id=1, source_target_pairs={{0,10},{2,12},{4,14},{6,16},{8,18},{10,20},{12,22},{14,24},{16,26}... | collective-permute-start | bytes 663560 | tf_op jit(solution)/shard_map/ppermute | solution.py:23
  1113.5 37.5 %collective-permute-start.46 = (bf16[288,384]{1,0:T(8,128)(2,1)}, bf16[288,384]{1,0:T(8,128)(2,1)S(1)}, u32[]{:S(2)}, u32[]{:S(2)}) collective-permute-start(bf16[288,384]{1,0:T(8,128)(2,1)} %get-tuple-element.695), channel_id=1, source_target_pairs={{0,8},{2,10},{4,12},{6,14},{8,16},{10,18},{12,20},{14,22},{16,24},... | collective-permute-start | bytes 663560 | tf_op jit(solution)/shard_map/ppermute | solution.py:23
  1114.2 37.2 %collective-permute-start.47 = (bf16[288,384]{1,0:T(8,128)(2,1)}, bf16[288,384]{1,0:T(8,128)(2,1)S(1)}, u32[]{:S(2)}, u32[]{:S(2)}) collective-permute-start(bf16[288,384]{1,0:T(8,128)(2,1)} %get-tuple-element.694), channel_id=1, source_target_pairs={{0,6},{2,8},{4,10},{6,12},{8,14},{10,16},{12,18},{14,20},{16,22},{... | collective-permute-start | bytes 663560 | tf_op jit(solution)/shard_map/ppermute | solution.py:23
  1117.1 35.9 %collective-permute-start.48 = (bf16[288,384]{1,0:T(8,128)(2,1)}, bf16[288,384]{1,0:T(8,128)(2,1)S(1)}, u32[]{:S(2)}, u32[]{:S(2)}) collective-permute-start(bf16[288,384]{1,0:T(8,128)(2,1)} %get-tuple-element.693), channel_id=1, source_target_pairs={{0,4},{2,6},{4,8},{6,10},{8,12},{10,14},{12,16},{14,18},{16,20},{1... | collective-permute-start | bytes 663560 | tf_op jit(solution)/shard_map/ppermute | solution.py:23
  (126 other events, 2699.3 us)
Sparse Core Ops, SparseCore 0:
  121.7 11.0 all-gather.4
  276.9 18.9 reduce-scatter.11
  320.1 16.4 all-gather.6
  407.9 20.3 reduce-scatter.13
  652.2 11.2 all-gather.8
  704.8 20.3 reduce-scatter.15
  750.0 16.3 all-gather.10
  772.5 107.9 all-reduce.6
  958.4 20.3 reduce-scatter.17
  985.2 170.4 reduce-scatter.31
  1161.5 151.9 reduce-scatter.29
  1319.4 122.6 reduce-scatter.27
  1448.2 122.5 reduce-scatter.21
  1576.7 122.5 reduce-scatter.23
  1705.1 122.5 reduce-scatter.25
  1833.6 121.2 reduce-scatter.19
where the time goes:
time: 1970 us; the launch traced here: 1960 us
  waiting for transfers between devices  1000 us (51%)
  matrix products  378 us (19%)
  local copies, waits for them, and re-layouts  226 us (11%)
  other arithmetic  125 us (6%)
  starting transfers between devices  114 us (6%)
  blocking collectives  102 us (5%)
    reduce_scatter x1, waiting for transfers between devices, body(): lax.psum_scatter(dw_inner, 'dp', scatter_dimension=0, tiled=True)  143 us
    reduce_scatter x1, waiting for transfers between devices, body(): lax.psum_scatter(dw_query, 'dp', scatter_dimension=0, tiled=True)  129 us
    reduce_scatter x1, waiting for transfers between devices, body(): lax.psum_scatter(dw_out, 'dp', scatter_dimension=1, tiled=True)  129 us
    reduce_scatter x1, waiting for transfers between devices, body(): lax.psum_scatter(dw_value, 'dp', scatter_dimension=0, tiled=True)  129 us
    reduce_scatter x1, waiting for transfers between devices, body(): lax.psum_scatter(dw_key, 'dp', scatter_dimension=0, tiled=True)  128 us
    reduce_scatter x1, waiting for transfers between devices, body(): lax.psum_scatter(grad_pos_part, 'dp', scatter_dimension=0, tiled=True)  127 us
    ppermute x55, waiting for transfers between devices, from_behind(): return lax.ppermute(value, axis, pairs)  113 us
    ppermute x55, starting transfers between devices, from_behind(): return lax.ppermute(value, axis, pairs)  112 us
  transfers between devices with their start and end apart: 71, of which 31 were waited for; matrix products, arithmetic and copies ran while one was open for 18% of the time, Pallas kernels for 0%

commit v1 on v0

v1 whole, which is shorter than its diff:
```python
import functools

import jax
import jax.numpy as jnp
from jax import lax
from jax.experimental import pallas as pl
from jax.experimental.pallas import tpu as pltpu
from jax.sharding import PartitionSpec as P

HEAD_DIM = 64
PROJ = 128
REACH = 6
SLOTS = 2 * REACH
EPSILON = 1e-05
NEGATIVE = -1e30
PRECISE = lax.Precision.HIGHEST
MESH = pl.DeviceIdType.MESH
BF = jnp.bfloat16
F32 = jnp.float32
VMEM_LIMIT = 60 * 1024 * 1024
VQ, VV, VO, VGA, VSA, VBO, VGF, VSF, VIN = range(9)
VROWS = 16


def any_spec(count):
    return [pl.BlockSpec(memory_space=pl.ANY)] * count


def vmem_spec(count):
    return [pl.BlockSpec(memory_space=pltpu.VMEM)] * count


def nt(left, right):
    return lax.dot_general(left, right, (((1,), (1,)), ((), ())), preferred_element_type=F32)


def tn(left, right):
    return lax.dot_general(left, right, (((0,), (0,)), ((), ())), preferred_element_type=F32)


def mm(left, right):
    return jnp.dot(left, right, preferred_element_type=F32)


def greet(targets):
    barrier = pltpu.get_barrier_semaphore()
    for target in targets:
        pl.semaphore_signal(barrier, inc=1, device_id=target, device_id_type=MESH)
    pl.semaphore_wait(barrier, len(targets))


def ring_partners(me, core, n):
    return [(lax.rem(me + step + n, n), core) for step in range(-REACH, REACH + 1) if step != 0]


def fetch_kernel(
    n, req, docs_in, tok_in, cot_in, wq_in, wk_in, wv_in, wo_in, wi_in, wu_in, wc_in, pos_in, vec_in,
    docs, tok, cot, wqkv, wo, wi, wu, wc, pos, vec, got,
    doc_buf, stage, got_s,
    req_send, req_recv, doc_send, doc_recv, fwd_send, fwd_recv, own_sem, sib_send, sib_recv, misc_sem,
):
    me = lax.axis_index("dp")
    core = lax.axis_index("mp")
    other = 1 - core
    sibling = (me, other)
    greet(ring_partners(me, core, n) + [sibling])
    half = tok_in.shape[2]
    rows = tok_in.shape[0] // 2
    inner = wi_in.shape[1]
    mine = pl.ds(pl.multiple_of(core * half, half), half)
    asked = []
    for slot in range(SLOTS):
        if slot == REACH:
            asked.append(None)
            continue
        copy = pltpu.make_async_remote_copy(
            src_ref=req.at[slot], dst_ref=got.at[slot], send_sem=req_send.at[slot],
            recv_sem=req_recv.at[slot],
            device_id=(lax.rem(me + slot - REACH + n, n), core), device_id_type=MESH,
        )
        copy.start()
        asked.append(copy)
    load = pltpu.make_async_copy(docs_in, doc_buf, misc_sem.at[0])
    load.start()
    pairs = [
        (tok_in.at[pl.ds(core * rows, rows)], tok_in.at[pl.ds(other * rows, rows)], tok.at[:, :, mine]),
        (cot_in.at[0], cot_in.at[0], cot.at[:, mine]),
        (pos_in, pos_in, pos.at[:, mine]),
        (vec_in, vec_in, vec.at[core]),
    ]
    for index, source in enumerate((wq_in, wk_in, wv_in)):
        begin = pl.multiple_of(index * 2 * half + core * half, half)
        pairs.append((source, source, wqkv.at[:, pl.ds(begin, half)]))
    pairs += [
        (wo_in, wo_in, wo.at[mine]),
        (wi_in, wi_in, wi.at[:, pl.ds(pl.multiple_of(core * inner, inner), inner)]),
        (wu_in, wu_in, wu.at[pl.ds(pl.multiple_of(core * inner, inner), inner)]),
        (wc_in, wc_in, wc.at[mine]),
    ]
    moves = []
    for index, (own_src, sib_src, dst) in enumerate(pairs):
        far = pltpu.make_async_remote_copy(
            src_ref=sib_src, dst_ref=dst, send_sem=sib_send.at[index], recv_sem=sib_recv.at[index],
            device_id=sibling, device_id_type=MESH,
        )
        far.start()
        near = pltpu.make_async_copy(own_src, dst, own_sem.at[index])
        near.start()
        moves += [far, near]
    got[REACH] = req[REACH]
    for copy in asked:
        if copy is not None:
            copy.wait_recv()
    to_scalar = pltpu.make_async_copy(got, got_s, misc_sem.at[1])
    to_scalar.start()
    load.wait()
    to_scalar.wait()
    sent = [None] * SLOTS
    order = sorted(range(SLOTS), key=lambda s: -abs(s - REACH))
    for slot in order:
        stage[slot] = doc_buf[jnp.maximum(got_s[slot, 0, 0], 0)]
        if slot == REACH:
            copy = pltpu.make_async_copy(stage.at[slot], docs.at[slot, :, mine], misc_sem.at[2])
        else:
            copy = pltpu.make_async_remote_copy(
                src_ref=stage.at[slot], dst_ref=docs.at[slot, :, mine], send_sem=doc_send.at[slot],
                recv_sem=doc_recv.at[slot],
                device_id=(lax.rem(me - slot + REACH + n, n), core), device_id_type=MESH,
            )
        copy.start()
        sent[slot] = copy
    passed = []
    for slot in reversed(order):
        if slot == REACH:
            sent[slot].wait()
        else:
            sent[slot].wait_recv()
        copy = pltpu.make_async_remote_copy(
            src_ref=docs.at[slot, :, mine], dst_ref=docs.at[slot, :, mine], send_sem=fwd_send.at[slot],
            recv_sem=fwd_recv.at[slot], device_id=sibling, device_id_type=MESH,
        )
        copy.start()
        passed.append(copy)
    for copy in moves + passed:
        copy.wait()
    for slot in range(SLOTS):
        if slot != REACH:
            asked[slot].wait_send()
            sent[slot].wait_send()


def fetch(n, req, doc_store, tokens, cot, wq, wk, wv, wo, wi, wu, wc, pos, vec):
    rows, seq, half = tokens.shape
    full = 2 * half
    inner = wi.shape[1]
    shape = jax.ShapeDtypeStruct
    out_shape = (
        shape((SLOTS, seq, full), BF),
        shape((rows // 2, seq, full), BF),
        shape((seq, full), BF),
        shape((full, 3 * full), BF),
        shape((full, full), BF),
        shape((full, 2 * inner), BF),
        shape((2 * inner, full), BF),
        shape((full, wc.shape[1]), BF),
        shape((pos.shape[0], full), BF),
        shape((2,) + vec.shape, F32),
        shape(req.shape, jnp.int32),
    )
    dma = pltpu.SemaphoreType.DMA
    return pl.pallas_call(
        functools.partial(fetch_kernel, n),
        out_shape=out_shape,
        in_specs=vmem_spec(1) + any_spec(12),
        out_specs=tuple(any_spec(10) + vmem_spec(1)),
        scratch_shapes=[
            pltpu.VMEM(doc_store.shape, BF),
            pltpu.VMEM((SLOTS, seq, half), BF),
            pltpu.SMEM(req.shape, jnp.int32),
            dma((SLOTS,)), dma((SLOTS,)), dma((SLOTS,)), dma((SLOTS,)), dma((SLOTS,)), dma((SLOTS,)),
            dma((11,)), dma((11,)), dma((11,)), dma((3,)),
        ],
        compiler_params=pltpu.CompilerParams(
            collective_id=0, has_side_effects=True, vmem_limit_bytes=VMEM_LIMIT
        ),
        name="fetch",
    )(req, doc_store, tokens, cot, wq, wk, wv, wo, wi, wu, wc, pos, vec)


def wide(vec, row):
    return jnp.concatenate([vec[0, row:row + 1, :], vec[1, row:row + 1, :]], axis=1)


def inner_bias(vec):
    return jnp.concatenate([vec[h, VIN + j:VIN + j + 1, :] for h in range(2) for j in range(4)], axis=1)


def normalize(hidden):
    average = jnp.mean(hidden, axis=-1, keepdims=True)
    centered = hidden - average
    spread = jnp.mean(centered * centered, axis=-1, keepdims=True)
    inverse = lax.rsqrt(spread + EPSILON)
    return centered * inverse, inverse


def head_masks():
    lane = lax.broadcasted_iota(jnp.int32, (1, 2 * HEAD_DIM), 1)
    first = (lane < HEAD_DIM).astype(F32)
    return [first.astype(BF), (1.0 - first).astype(BF)]


def forward_kernel(
    slot_ref, tok, doc, place, seg_col, seg_row, pos, wqkv, wo, wi, wu, wc, vec, cot,
    xlow, qkv, lse, ctx, nmid, imid, mlow, act, slope, nout, iout, res, summ, prod,
    bias, stats, acc,
):
    seq, full = tok.shape[1], tok.shape[2]
    table = pos.shape[0]
    one_hot = (place[0] == lax.broadcasted_iota(jnp.int32, (seq, table), 1)).astype(F32).astype(BF)
    embedded = tok[0].astype(F32) + mm(one_hot, pos[...]) + doc[0].astype(F32)
    low = embedded.astype(BF)
    xlow[0] = low
    acc[...] = embedded
    q = (mm(low, wqkv[:, 0:full]) + wide(vec, VQ)).astype(BF)
    qkv[0, :, 0:full] = q * jnp.asarray(HEAD_DIM ** -0.5, BF)
    qkv[0, :, full:2 * full] = mm(low, wqkv[:, full:2 * full]).astype(BF)
    qkv[0, :, 2 * full:] = (mm(low, wqkv[:, 2 * full:]) + wide(vec, VV)).astype(BF)
    bias[...] = jnp.where(seg_col[0] == seg_row[0], 0.0, NEGATIVE)
    masks = head_masks()
    pair = 2 * HEAD_DIM
    stats[...] = jnp.zeros_like(stats)

    def heads(p, carry):
        at = pl.multiple_of(p * pair, pair)
        queries = qkv[0, :, pl.ds(at, pair)]
        keys = qkv[0, :, pl.ds(full + at, pair)]
        values = qkv[0, :, pl.ds(2 * full + at, pair)]
        lane = lax.broadcasted_iota(jnp.int32, (seq, pair), 1)
        parts = []
        for h in range(2):
            s = nt(queries * masks[h], keys) + bias[...]
            top = jnp.max(s, axis=1, keepdims=True)
            e = jnp.exp(s - top)
            total = jnp.sum(e, axis=1, keepdims=True)
            parts.append(mm((e * (1.0 / total)).astype(BF), values))
            stats[0:seq, :] = jnp.where(lane == 2 * p + h, top + jnp.log(total), stats[0:seq, :])
        ctx[0, :, pl.ds(at, pair)] = jnp.where(lane < HEAD_DIM, parts[0], parts[1]).astype(BF)
        return carry

    lax.fori_loop(0, full // pair, heads, 0)
    lse[0] = jnp.transpose(stats[...])[0:lse.shape[1], 0:seq]
    normed, inverse = normalize(acc[...] + mm(ctx[0], wo[...]) + wide(vec, VO))
    middle = normed * wide(vec, VGA) + wide(vec, VSA)
    nmid[0] = normed.astype(BF)
    imid[0] = inverse
    acc[...] = middle + wide(vec, VBO)
    mlow[0] = middle.astype(BF)
    hidden = wi.shape[1]
    chunk = hidden // 4
    bin_all = inner_bias(vec)
    for j in range(4):
        cols = slice(j * chunk, (j + 1) * chunk)
        pre = mm(mlow[0], wi[:, cols]) + bin_all[:, cols]
        phi = 0.5 + 0.5 * lax.erf(pre * (0.5 ** 0.5))
        act[0, :, cols] = (pre * phi).astype(BF)
        slope[0, :, cols] = (phi + pre * (jnp.exp(-0.5 * pre * pre) * 0.3989422804014327)).astype(BF)
        acc[...] += mm(act[0, :, cols], wu[cols, :])
    normed, inverse = normalize(acc[...])
    nout[0] = normed.astype(BF)
    iout[0] = inverse
    result = (normed * wide(vec, VGF) + wide(vec, VSF)).astype(BF)
    res[0] = result
    summ[0] = mm(res[0, 0:16, :], wc[...])[0:8]
    product = jnp.sum(cot[...].astype(F32) * result.astype(F32))
    prod[0] = jnp.full(prod.shape[1:], product, F32)


def forward(slots, tok, docs, place, seg_col, seg_row, pos, wqkv, wo, wi, wu, wc, vec, cot):
    rows, seq, full = tok.shape
    hidden = wi.shape[1]
    shape = jax.ShapeDtypeStruct
    heads = full // HEAD_DIM
    lse_rows = (heads + 7) // 8 * 8

    def row_block(*dims):
        return pl.BlockSpec((1,) + dims, lambda b, s: (b,) + (0,) * len(dims))

    def whole(*dims):
        return pl.BlockSpec(dims, lambda b, s: (0,) * len(dims), pipeline_mode=pl.Buffered(1))

    outs = [
        ((seq, full), BF), ((seq, 3 * full), BF), ((lse_rows, seq), F32), ((seq, full), BF),
        ((seq, full), BF), ((seq, 1), F32), ((seq, full), BF), ((seq, hidden), BF), ((seq, hidden), BF),
        ((seq, full), BF), ((seq, 1), F32), ((seq, full), BF), ((8, PROJ), F32), ((8, PROJ), F32),
    ]
    return pl.pallas_call(
        forward_kernel,
        out_shape=tuple(shape((rows,) + dims, kind) for dims, kind in outs),
        grid_spec=pltpu.PrefetchScalarGridSpec(
            num_scalar_prefetch=1,
            grid=(rows,),
            in_specs=[
                row_block(seq, full),
                pl.BlockSpec((1, seq, full), lambda b, s: (s[b], 0, 0)),
                row_block(seq, 1), row_block(seq, 1), row_block(1, seq),
                whole(*pos.shape), whole(*wqkv.shape), whole(*wo.shape), whole(*wi.shape),
                whole(*wu.shape), whole(*wc.shape), whole(*vec.shape), whole(*cot.shape),
            ],
            out_specs=tuple(row_block(*dims) for dims, _ in outs),
            scratch_shapes=[
                pltpu.VMEM((seq, seq), F32), pltpu.VMEM((384, 128), F32), pltpu.VMEM((seq, full), F32),
            ],
        ),
        compiler_params=pltpu.CompilerParams(vmem_limit_bytes=VMEM_LIMIT),
        name="forward",
    )(slots, tok, docs, place, seg_col, seg_row, pos, wqkv, wo, wi, wu, wc, vec, cot)


def shares_kernel(summ, prod, qv, shares, dsum, gq, mine, theirs, send_sem, recv_sem):
    me = lax.axis_index("dp")
    core = lax.axis_index("mp")
    sibling = (me, 1 - core)
    greet([sibling])
    rows = summ.shape[0]
    mine[...] = jnp.concatenate([summ[b, 0:1, :] for b in range(rows)] + [prod[b, 0:1, :] for b in range(rows)], axis=0)
    copy = pltpu.make_async_remote_copy(
        src_ref=mine, dst_ref=theirs, send_sem=send_sem, recv_sem=recv_sem,
        device_id=sibling, device_id_type=MESH,
    )
    copy.start()
    copy.wait()
    first = core == 0
    low = jnp.where(first, mine[...], theirs[...])
    high = jnp.where(first, theirs[...], mine[...])
    summary = jnp.concatenate([low[:rows], high[:rows]], axis=0)
    product = jnp.concatenate([low[rows:], high[rows:]], axis=0)
    inv_root = PROJ ** (-0.5)
    logits = jnp.sum(summary * qv[...], axis=1, keepdims=True) * inv_root
    e = jnp.exp(logits - jnp.max(logits, axis=0, keepdims=True))
    share = e / jnp.sum(e, axis=0, keepdims=True)
    dlogits = share * (product - jnp.sum(share * product, axis=0, keepdims=True))
    gq[...] = jnp.sum(dlogits * summary, axis=0, keepdims=True) * inv_root
    ds = dlogits * qv[...] * inv_root
    wide_share = share + jnp.zeros_like(ds)
    shares[...] = jnp.where(first, wide_share, jnp.concatenate([wide_share[rows:], wide_share[:rows]], axis=0))
    dsum[...] = jnp.where(first, ds, jnp.concatenate([ds[rows:], ds[:rows]], axis=0))


def share_out(summ, prod, qv):
    rows = summ.shape[0]
    shape = jax.ShapeDtypeStruct
    return pl.pallas_call(
        shares_kernel,
        out_shape=(shape((2 * rows, PROJ), F32), shape((2 * rows, PROJ), F32), shape((1, PROJ), F32)),
        in_specs=vmem_spec(3),
        out_specs=tuple(vmem_spec(3)),
        scratch_shapes=[
            pltpu.VMEM((2 * rows, PROJ), F32), pltpu.VMEM((2 * rows, PROJ), F32),
            pltpu.SemaphoreType.DMA, pltpu.SemaphoreType.DMA,
        ],
        compiler_params=pltpu.CompilerParams(collective_id=1, has_side_effects=True),
        name="shares",
    )(summ, prod, qv)


def norm_back(upstream, normed, inverse, gain):
    scaled = upstream * gain
    first = jnp.mean(scaled, axis=-1, keepdims=True)
    second = jnp.mean(scaled * normed, axis=-1, keepdims=True)
    return inverse * (scaled - first - normed * second)


def add_vec(vecs, row, value):
    half = value.shape[1] // 2
    vecs[0, row:row + 1, :] += value[:, :half]
    vecs[1, row:row + 1, :] += value[:, half:]


def token_sum(values):
    return jnp.sum(values, axis=0, keepdims=True)


def backward_kernel(
    shares, dsum, cot, res, nout, iout, slope, nmid, imid, qkv, lse, seg_col, seg_row,
    wqkv, wo, wi, wu, wc, vec,
    douter, dinner, dattn, dqkv, dstart, mixed, vecs,
    bias, grads, acc,
):
    b = pl.program_id(0)
    seq, full = cot.shape
    half = full // 2
    hidden = wi.shape[1]

    @pl.when(b == 0)
    def _():
        mixed[...] = jnp.zeros_like(mixed)
        vecs[...] = jnp.zeros_like(vecs)

    share = shares[pl.ds(b, 1), 0:1]
    mixed[...] += share * res[0].astype(F32)
    extra = lax.dot_general(
        jnp.broadcast_to(dsum[pl.ds(b, 1), :], (8, PROJ)), wc[...].astype(F32), (((1,), (1,)), ((), ())),
        preferred_element_type=F32, precision=PRECISE,
    )[0:1]
    row = lax.broadcasted_iota(jnp.int32, (seq, 1), 0)
    upstream = share * cot[...].astype(F32) + jnp.where(row == 0, extra, 0.0)
    upstream = upstream.astype(BF).astype(F32)
    normed = nout[0].astype(F32)
    dout = norm_back(upstream, normed, iout[0], wide(vec, VGF))
    add_vec(vecs, VGF, token_sum(upstream * normed))
    add_vec(vecs, VSF, token_sum(upstream))
    add_vec(vecs, VBO, token_sum(dout))
    douter[0] = dout.astype(BF)
    acc[...] = dout
    chunk = hidden // 4
    for j in range(4):
        cols = slice(j * chunk, (j + 1) * chunk)
        part = nt(douter[0], wu[cols, :]) * slope[0, :, cols].astype(F32)
        dinner[0, :, cols] = part.astype(BF)
        sums = token_sum(part)
        for i in range(2):
            quarter = 2 * j + i
            vecs[quarter // 4, VIN + quarter % 4:VIN + quarter % 4 + 1, :] += sums[:, i * half:(i + 1) * half]
        acc[...] += nt(dinner[0, :, cols], wi[:, cols])
    upstream = acc[...]
    normed = nmid[0].astype(F32)
    dmid = norm_back(upstream, normed, imid[0], wide(vec, VGA))
    add_vec(vecs, VGA, token_sum(upstream * normed))
    add_vec(vecs, VSA, token_sum(upstream))
    add_vec(vecs, VO, token_sum(dmid))
    dattn[0] = dmid.astype(BF)
    acc[...] = dmid
    grads[:, 0:full] = nt(dattn[0], wo[...]).astype(BF)
    bias[...] = jnp.where(seg_col[0] == seg_row[0], 0.0, NEGATIVE)
    masks = head_masks()
    pair = 2 * HEAD_DIM
    per_half = half // pair

    def heads(p, carry):
        at = pl.multiple_of(p * pair, pair)
        out_at = pl.multiple_of((p // per_half) * (3 * half) + (p % per_half) * pair, pair)
        queries = qkv[0, :, pl.ds(at, pair)]
        keys = qkv[0, :, pl.ds(full + at, pair)]
        values = qkv[0, :, pl.ds(2 * full + at, pair)]
        dctx = grads[:, pl.ds(at, pair)]
        lane = lax.broadcasted_iota(jnp.int32, (seq, pair), 1)
        parts = []
        for h in range(2):
            s = nt(keys * masks[h], queries) + bias[...]
            w = jnp.exp(s - lse[0, pl.ds(2 * p + h, 1), :])
            dv = mm(w.astype(BF), dctx)
            prod = w * nt(values * masks[h], dctx)
            ds = (prod - w * token_sum(prod)).astype(BF)
            dk = mm(ds, queries)
            dq = tn(ds, keys) * HEAD_DIM ** -0.5
            parts.append((dq, dk, dv))
        for t in range(3):
            joined = jnp.where(lane < HEAD_DIM, parts[0][t], parts[1][t]).astype(BF)
            dqkv[0, :, pl.ds(out_at + t * half, pair)] = joined
        return carry

    lax.fori_loop(0, full // pair, heads, 0)
    total = acc[...]
    for h in range(2):
        for t in range(3):
            source = dqkv[0, :, (3 * h + t) * half:(3 * h + t + 1) * half]
            total += nt(source, wqkv[:, t * full + h * half:t * full + (h + 1) * half])
            if t != 1:
                at = VQ if t == 0 else VV
                vecs[h, at:at + 1, :] += token_sum(source.astype(F32))
    dstart[0] = total.astype(BF)


def backward(shares, dsum, cot, res, nout, iout, slope, nmid, imid, qkv, lse, seg_col, seg_row, wqkv, wo, wi, wu, wc, vec):
    rows, seq, full = res.shape
    hidden = wi.shape[1]
    shape = jax.ShapeDtypeStruct

    def row_block(array):
        dims = array.shape[1:]
        return pl.BlockSpec((1,) + dims, lambda b: (b,) + (0,) * len(dims))

    def whole(array):
        dims = array.shape
        return pl.BlockSpec(dims, lambda b: (0,) * len(dims), pipeline_mode=pl.Buffered(1))

    outs = (
        shape((rows, seq, full), BF), shape((rows, seq, hidden), BF), shape((rows, seq, full), BF),
        shape((rows, seq, 3 * full), BF), shape((rows, seq, full), BF),
    )
    sums = (shape((seq, full), F32), shape((2, VROWS, full // 2), F32))
    by_row = (res, nout, iout, slope, nmid, imid, qkv, lse, seg_col, seg_row)
    fixed = (wqkv, wo, wi, wu, wc, vec)
    return pl.pallas_call(
        backward_kernel,
        out_shape=outs + sums,
        grid=(rows,),
        in_specs=[whole(shares), whole(dsum), whole(cot)] + [row_block(a) for a in by_row] + [whole(a) for a in fixed],
        out_specs=tuple([row_block(a) for a in outs] + [whole(a) for a in sums]),
        scratch_shapes=[
            pltpu.VMEM((seq, seq), F32), pltpu.VMEM((seq, full), BF), pltpu.VMEM((seq, full), F32),
        ],
        compiler_params=pltpu.CompilerParams(vmem_limit_bytes=VMEM_LIMIT),
        name="backward",
    )(shares, dsum, cot, *by_row, *fixed)


def with_bit(index, position, bit):
    low = 1 << position
    return (index // low) * (2 * low) + bit * low + index % low


def reduce_kernel(n, groups, mats, *refs):
    refs = list(refs)

    def take(count):
        taken = refs[:count]
        del refs[:count]
        return taken

    slot_row, vec_in, mixed_in, dstart = take(4)
    grads_in = take(mats)
    gt, arrived, mixed, vec_out = take(4)
    grads_out = take(mats)
    gt_v, stage, mix_own, mix_got, vec_bufs = take(5)
    levels = n.bit_length() - 1
    bufs = [take(2 + 3 * levels) for _ in groups]
    (own_sem, sib_send, sib_recv, doc_send, doc_recv, vec_send, vec_recv, m_sem, m_send, m_recv, x_send, x_recv) = take(12)
    me = lax.axis_index("dp")
    core = lax.axis_index("mp")
    other = 1 - core
    sibling = (me, other)

    def across(bit):
        here = (me // (1 << bit)) % 2
        return here, (me + (1 - 2 * here) * (1 << bit), core)

    far = [across(bit)[1] for bit in range(levels) if (1 << bit) > REACH]
    greet(ring_partners(me, core, n) + [sibling] + (far if mats else []))
    rows, seq, full = dstart.shape
    half = full // 2
    here_cols = pl.ds(pl.multiple_of(core * half, half), half)
    there_cols = pl.ds(pl.multiple_of(other * half, half), half)
    my_rows = pl.ds(core * rows, rows)

    tok_far = pltpu.make_async_remote_copy(
        src_ref=dstart.at[:, :, there_cols], dst_ref=gt_v.at[my_rows], send_sem=sib_send.at[0],
        recv_sem=sib_recv.at[0], device_id=sibling, device_id_type=MESH,
    )
    tok_far.start()
    tok_own = pltpu.make_async_copy(dstart.at[:, :, here_cols], gt_v.at[my_rows], own_sem.at[0])
    tok_own.start()
    mix_far = pltpu.make_async_remote_copy(
        src_ref=mixed_in.at[:, there_cols], dst_ref=mix_got, send_sem=sib_send.at[1],
        recv_sem=sib_recv.at[1], device_id=sibling, device_id_type=MESH,
    )
    mix_far.start()
    mix_load = pltpu.make_async_copy(mixed_in.at[:, here_cols], mix_own, own_sem.at[1])
    mix_load.start()
    vec_copy = pltpu.make_async_remote_copy(
        src_ref=vec_in.at[other], dst_ref=vec_bufs.at[0], send_sem=vec_send.at[0],
        recv_sem=vec_recv.at[0], device_id=sibling, device_id_type=MESH,
    )
    vec_copy.start()

    first = []
    for g, (mat, begin, width, _) in enumerate(groups):
        half_width = grads_in[mat].shape[2] // 2
        mine, theirs = bufs[g][0], bufs[g][1]
        there = pl.ds(pl.multiple_of(other * half_width + begin, 128), width)
        here = pl.ds(pl.multiple_of(core * half_width + begin, 128), width)
        send = pltpu.make_async_remote_copy(
            src_ref=grads_in[mat].at[:, :, there], dst_ref=theirs, send_sem=m_send.at[g],
            recv_sem=m_recv.at[g], device_id=sibling, device_id_type=MESH,
        )
        send.start()
        load = pltpu.make_async_copy(grads_in[mat].at[:, :, here], mine, m_sem.at[g])
        load.start()
        first.append((send, load))

    tok_own.wait()
    tok_far.wait()
    tok_out = pltpu.make_async_copy(gt_v, gt, own_sem.at[2])
    tok_out.start()
    sent = []
    order = sorted(range(SLOTS), key=lambda s: -abs(s - REACH))
    for slot in order:
        stage[slot] = gt_v[slot_row[slot]]
        if slot == REACH:
            copy = pltpu.make_async_copy(stage.at[slot], arrived.at[slot], own_sem.at[3])
        else:
            copy = pltpu.make_async_remote_copy(
                src_ref=stage.at[slot], dst_ref=arrived.at[slot], send_sem=doc_send.at[slot],
                recv_sem=doc_recv.at[slot],
                device_id=(lax.rem(me + slot - REACH + n, n), core), device_id_type=MESH,
            )
        copy.start()
        sent.append(copy)

    pending = [None] * len(groups)
    vec_total = None
    for level in range(levels + 1):
        for g, (mat, begin, width, bits) in enumerate(groups):
            base = bufs[g]
            if level == 0:
                for copy in first[g]:
                    copy.wait()
                held, came = base[0], base[1]
            else:
                pending[g].wait()
                held, came = base[2 + 3 * (level - 1) + 1], base[2 + 3 * (level - 1) + 2]
            if level == levels:
                grads_out[mat][:, begin:begin + width] = held[0].astype(F32) + came[0].astype(F32)
                continue
            to_send, to_keep, to_get = base[2 + 3 * level:5 + 3 * level]
            bit = bits[level]
            place = sum(1 for earlier in range(bit) if earlier not in bits[:level])
            here, partner = across(bit)

            def add(t, carry, held=held, came=came, to_send=to_send, to_keep=to_keep, place=place, here=here):
                gone = with_bit(t, place, 1 - here)
                kept = with_bit(t, place, here)
                to_send[t] = (held[gone].astype(F32) + came[gone].astype(F32)).astype(BF)
                to_keep[t] = (held[kept].astype(F32) + came[kept].astype(F32)).astype(BF)
                return carry

            lax.fori_loop(0, n >> (level + 1), add, 0)
            pending[g] = pltpu.make_async_remote_copy(
                src_ref=to_send, dst_ref=to_get, send_sem=x_send.at[g, level], recv_sem=x_recv.at[g, level],
                device_id=partner, device_id_type=MESH,
            )
            pending[g].start()
        if mats:
            vec_copy.wait()
            if level == 0:
                vec_total = vec_in[core] + vec_bufs[0]
            else:
                vec_total = vec_total + vec_bufs[2 * level]
            if level < levels:
                vec_bufs[2 * level + 1] = vec_total
                vec_copy = pltpu.make_async_remote_copy(
                    src_ref=vec_bufs.at[2 * level + 1], dst_ref=vec_bufs.at[2 * level + 2],
                    send_sem=vec_send.at[level + 1], recv_sem=vec_recv.at[level + 1],
                    device_id=across(level)[1], device_id_type=MESH,
                )
                vec_copy.start()
            else:
                vec_out[...] = vec_total
    if not mats:
        vec_copy.wait()
        vec_out[...] = vec_in[core] + vec_bufs[0]
    mix_load.wait()
    mix_far.wait()
    mixed[...] = (mix_own[...] + mix_got[...]).astype(BF)
    tok_out.wait()
    for copy in sent:
        copy.wait()


def deliver(n, groups, slot_row, vecs, mixed, dstart, grads):
    rows, seq, full = dstart.shape
    half = full // 2
    levels = n.bit_length() - 1
    shape = jax.ShapeDtypeStruct
    outs = [
        shape((2 * rows, seq, half), BF), shape((SLOTS, seq, half), BF), shape((seq, half), BF),
        shape(vecs.shape[1:], F32),
    ] + [shape((g.shape[1], g.shape[2] // 2), F32) for g in grads]
    scratch = [
        pltpu.VMEM((2 * rows, seq, half), BF), pltpu.VMEM((SLOTS, seq, half), BF),
        pltpu.VMEM((seq, half), F32), pltpu.VMEM((seq, half), F32),
        pltpu.VMEM((2 * levels + 2,) + vecs.shape[1:], F32),
    ]
    for mat, _, width, _ in groups:
        depth = grads[mat].shape[1]
        scratch += [pltpu.VMEM((n, depth, width), BF)] * 2
        for level in range(levels):
            scratch += [pltpu.VMEM((n >> (level + 1), depth, width), BF)] * 3
    dma = pltpu.SemaphoreType.DMA
    count = max(1, len(groups))
    scratch += [
        dma((4,)), dma((2,)), dma((2,)), dma((SLOTS,)), dma((SLOTS,)), dma((levels + 1,)), dma((levels + 1,)),
        dma((count,)), dma((count,)), dma((count,)), dma((count, levels)), dma((count, levels)),
    ]
    return pl.pallas_call(
        functools.partial(reduce_kernel, n, groups, len(grads)),
        out_shape=tuple(outs),
        in_specs=[pl.BlockSpec(memory_space=pltpu.SMEM)] + vmem_spec(1) + any_spec(2 + len(grads)),
        out_specs=tuple(any_spec(2) + vmem_spec(2 + len(grads))),
        scratch_shapes=scratch,
        compiler_params=pltpu.CompilerParams(
            collective_id=2, has_side_effects=True, vmem_limit_bytes=VMEM_LIMIT
        ),
        name="deliver",
    )(slot_row, vecs, mixed, dstart, *grads)


def place_kernel(want, arrived, out):
    d = pl.program_id(0)
    out[...] = jnp.zeros_like(out)
    for slot in range(SLOTS):

        @pl.when(want[slot] == d)
        def _(slot=slot):
            out[0] += arrived[slot].astype(F32)


def place_docs(want, arrived, docs):
    _, seq, half = arrived.shape
    return pl.pallas_call(
        place_kernel,
        out_shape=jax.ShapeDtypeStruct((docs, seq, half), F32),
        grid_spec=pltpu.PrefetchScalarGridSpec(
            num_scalar_prefetch=1,
            grid=(docs,),
            in_specs=[pl.BlockSpec(arrived.shape, lambda d, w: (0, 0, 0), pipeline_mode=pl.Buffered(1))],
            out_specs=pl.BlockSpec((1, seq, half), lambda d, w: (d, 0, 0)),
        ),
        compiler_params=pltpu.CompilerParams(vmem_limit_bytes=VMEM_LIMIT),
        name="place_docs",
    )(want, arrived)


def cut_groups(widths, levels):
    plain = tuple(range(levels))
    swapped = (1, 0) + plain[2:]
    groups = []
    for mat, width in enumerate(widths):
        begin = 0
        while begin < width:
            size = min(768, width - begin)
            groups.append((mat, begin, size, plain if len(groups) % 2 == 0 else swapped))
            begin += size
    return tuple(groups)


def body(
    tokens, segment_ids, positions, query_vectors, doc_owner, doc_slot, doc_store, pos_table,
    w_query, w_key, w_value, b_query, b_value, w_out, b_out, gain_attn, shift_attn,
    w_inner, b_inner, w_outer, b_outer, gain_ffn, shift_ffn, w_cls, cotangent,
):
    n = lax.axis_size("dp")
    me = lax.axis_index("dp")
    core = lax.axis_index("mp")
    row_count, seq, half = tokens.shape
    rows = row_count // 2
    full = 2 * half
    doc_count = doc_store.shape[0]
    place_slot = (doc_owner[0] - me + REACH) % n
    match = (place_slot[None, :] == jnp.arange(SLOTS, dtype=jnp.int32)[:, None]).astype(jnp.int32)
    req = jnp.sum(match * (doc_slot[0] + 1)[None, :], axis=1) - 1
    slot_row = jnp.sum(match * jnp.arange(row_count, dtype=jnp.int32)[None, :], axis=1)
    req = jnp.broadcast_to(req[:, None, None], (SLOTS, 8, 128))
    vec_in = jnp.concatenate(
        [v.reshape(-1, half) for v in (b_query, b_value, b_out, gain_attn, shift_attn, b_outer, gain_ffn, shift_ffn, b_inner)]
        + [jnp.zeros((VROWS - 12, half), F32)], axis=0,
    )
    docs, tok, cot, wqkv, wo, wi, wu, wc, pos, vec, got = fetch(
        n, req, doc_store, tokens, cotangent, w_query, w_key, w_value, w_out, w_inner, w_outer, w_cls, pos_table, vec_in
    )
    want = got[:, 0, 0]
    seg = lax.dynamic_slice_in_dim(segment_ids, core * rows, rows, 0)
    place = lax.dynamic_slice_in_dim(positions, core * rows, rows, 0)
    my_slots = lax.dynamic_slice_in_dim(place_slot, core * rows, rows, 0)
    seg_col, seg_row = seg[:, :, None], seg[:, None, :]
    xlow, qkv, lse, ctx, nmid, imid, mlow, act, slope, nout, iout, res, summ, prod = forward(
        my_slots, tok, docs, place[:, :, None], seg_col, seg_row, pos, wqkv, wo, wi, wu, wc, vec, cot
    )
    shares, dsum, grad_query = share_out(summ, prod, query_vectors)
    douter, dinner, dattn, dqkv, dstart, mixed, vecs = backward(
        shares, dsum, cot, res, nout, iout, slope, nmid, imid, qkv, lse, seg_col, seg_row, wqkv, wo, wi, wu, wc, vec
    )

    def cross(left, right):
        left = left.reshape(-1, left.shape[-1])
        right = right.reshape(-1, right.shape[-1])
        return tn(left, right)

    one_hot = (place.reshape(-1)[:, None] == jnp.arange(pos_table.shape[0], dtype=jnp.int32)[None, :]).astype(BF)
    dw_cls = lax.dot_general(
        dsum[:rows], res[:, 0, :].astype(F32), (((0,), (0,)), ((), ())), preferred_element_type=F32, precision=PRECISE
    )
    dpos = cross(one_hot, dstart)
    pieces = [cross(douter, act), cross(mlow, dinner), cross(dattn, ctx), cross(xlow, dqkv)]
    if full // n % 16 == 0:
        small = jnp.concatenate(
            [dw_cls.reshape(n, -1, full), dpos.reshape(n, -1, full)], axis=1
        )
        small = jnp.pad(small, ((0, 0), (0, full // n - small.shape[1]), (0, 0)))
        grads = [p.astype(BF).reshape(n, full // n, -1) for p in pieces] + [small.astype(BF)]
        groups = cut_groups([g.shape[2] // 2 for g in grads], n.bit_length() - 1)
        out = deliver(n, groups, slot_row, vecs, mixed, dstart, grads)
        grad_tokens, arrived, mixed_out, vec_sum = out[:4]
        g_outer, g_inner, g_wo, g_qkv, g_small = out[4:]
        g_cls = g_small[:PROJ // n]
        g_pos = g_small[PROJ // n:(PROJ + pos_table.shape[0]) // n]
    else:
        grad_tokens, arrived, mixed_out, vec_sum = deliver(n, (), slot_row, vecs, mixed, dstart, [])
        vec_sum = lax.psum(vec_sum, "dp")

        def scatter(part):
            part = lax.psum_scatter(part.astype(F32), "mp", scatter_dimension=1, tiled=True)
            return lax.psum_scatter(part, "dp", scatter_dimension=0, tiled=True)

        g_outer, g_inner, g_wo, g_qkv, g_cls, g_pos = [scatter(p) for p in pieces + [dw_cls, dpos]]
    grad_docs = place_docs(want, arrived, doc_count)

    def row(index):
        return vec_sum[index]

    return (
        mixed_out[None],
        grad_tokens,
        grad_query,
        grad_docs,
        g_pos,
        g_qkv[:, :half],
        g_qkv[:, half:2 * half],
        g_qkv[:, 2 * half:],
        row(VQ),
        row(VV),
        g_wo.T,
        row(VO),
        row(VGA),
        row(VSA),
        g_inner,
        vec_sum[VIN:VIN + 4].reshape(-1),
        g_outer.T,
        row(VBO),
        row(VGF),
        row(VSF),
        g_cls.T,
    )


def solution(mesh):
    rows = P("dp", None, "mp")
    ids = P("dp", None)
    cols = P(None, "mp")
    vec = P("mp")
    deep = P("mp", None)
    in_specs = (
        rows, ids, ids, ids, ids, ids, rows, cols, cols, cols, cols, vec, vec, deep, vec, vec, vec,
        cols, vec, deep, vec, vec, vec, deep, rows,
    )
    near = P("dp", "mp")
    turned = P("mp", "dp")
    out_specs = (
        rows, rows, ids, rows, near, near, near, near, vec, vec, turned, vec, vec, vec, near, vec,
        turned, vec, vec, vec, turned,
    )
    return jax.shard_map(body, mesh=mesh, in_specs=in_specs, out_specs=out_specs, check_vma=False)
```

time: 1970 us -> 601 us (0.31)
  waiting for transfers between devices: 1000 us -> 0 us
  Pallas kernels: 0 us -> 540 us
  matrix products: 378 us -> 28.3 us
  local copies, waits for them, and re-layouts: 226 us -> 27.6 us
  other arithmetic: 125 us -> 3.15 us
  starting transfers between devices: 114 us -> 0 us
  blocking collectives: 102 us -> 0 us
    reduce_scatter x11 -> x0, waiting for transfers between devices: 844 us -> none  [the longest x1 143 us: body(): lax.psum_scatter(dw_inner, 'dp', scatter_dimension=0, tiled=True)]
    pallas_call x0 -> x6, Pallas kernels: none -> 540 us  [the longest x1 274 us: fetch(): pl.pallas_call(functools.partial(fetch_kernel, n), out_shape=out_shape, i...]
    dot_general x71 -> x6, matrix products: 378 us -> 28.3 us  [the longest x5 27.9 us: tn(): lax.dot_general(left, right, (((0,), (0,)), ((), ())), preferred_element_...]
    ppermute x55 -> x0, waiting for transfers between devices: 113 us -> none  [from_behind(): return lax.ppermute(value, axis, pairs)]
    ppermute x55 -> x0, starting transfers between devices: 112 us -> none  [from_behind(): return lax.ppermute(value, axis, pairs)]
    psum x8 -> x0, blocking collectives: 102 us -> none  [the longest x1 78.4 us: body(): lax.psum((dbias_query, dbias_value, dbias_out, dgain_attn, dshift_attn, d...]
    reduce_sum x22 -> x1, other arithmetic: 69.5 us -> 0.59 us  [body(): req = jnp.sum(match * (doc_slot[0] + 1)[None, :], axis=1) - 1]
    another operation x33 -> x0, local copies, waits for them, and re-layouts: 54.2 us -> none  [the longest x14 29.6 us: carry_blocks(): return jnp.stack(moved)]
  transfers between devices with their start and end apart: 71 -> 0, of which waited for: 31 -> 0; matrix products, arithmetic and copies ran while one was open for 18% -> 0% of each run, Pallas kernels for 0% -> 0%
where the time goes in v1:
time: 601 us; the launch traced here: 600 us
  Pallas kernels  540 us (90%)
  matrix products  28.3 us (5%)
  local copies, waits for them, and re-layouts  27.6 us (5%)
    pallas_call x1, Pallas kernels, fetch(): pl.pallas_call(functools.partial(fetch_kernel, n), out_shape=out_shape, i...  274 us
    pallas_call x1, Pallas kernels, deliver(): pl.pallas_call(functools.partial(reduce_kernel, n, groups, len(grads)), o...  128 us
    pallas_call x1, Pallas kernels, backward(): pl.pallas_call(backward_kernel, out_shape=outs + sums, grid=(rows,), in_s...  66.4 us
    pallas_call x1, Pallas kernels, forward(): pl.pallas_call(forward_kernel, out_shape=tuple((shape((rows,) + dims, kin...  59.4 us
    dot_general x5, matrix products, tn(): lax.dot_general(left, right, (((0,), (0,)), ((), ())), preferred_element_...  27.9 us

profile of v1, /device:TPU:0, one launch (start us, length us, event | category | flops | bytes accessed | tf_op | source)
XLA Modules:
  0.0 600.2 jit_solution(1038388513704671841)
XLA Ops:
  3.2 0.7 reshape.124
  6.6 0.7 reshape.129
  7.3 0.7 reshape.130
  8.7 0.7 reshape.132
  9.4 1.2 concatenate.7.vec_in
  10.6 0.7 constant_dynamic-slice_fusion
  12.0 0.7 broadcast_in_dim.12.req
  12.7 1.1 copy.52.seg_col
  13.8 1.0 copy.51.place
  14.8 274.0 %fetch.1 = (bf16[12,288,768]{2,1,0:T(8,128)(2,1)}, bf16[4,288,768]{2,1,0:T(8,128)(2,1)}, bf16[288,768]{1,0:T(8,128)(2,1)}, bf16[768,2304]{1,0:T(8,128)(2,1)}, bf...) custom-call(s32[12,8,128]{2,1,0:T(8,128)} %broadcast_in_dim.12.req, ...), custom_call_target="tpu_custom_call" | custom-call | tf_op jit(solution)/shard_map/fetch/pallas_call | solution.py:171
  288.9 1.6 slice_reduce_fusion.want
  290.5 59.4 %forward.1 = (bf16[4,288,768]{2,1,0:T(8,128)(2,1)}, bf16[4,288,2304]{2,1,0:T(8,128)(2,1)}, f32[4,16,288]{2,1,0:T(8,128)}, bf16[4,288,768]{2,1,0:T(8,128)(2,1)}, ...) custom-call(s32[4]{0:T(128)} %dynamic_slice.9.slot_ref, ...), custom_call_target="tpu_custom_call" | custom-call | tf_op jit(solution)/shard_map/forward/pallas_call | solution.py:296
  349.9 2.6 shares.1
  352.6 66.4 %backward.1 = (bf16[4,288,768]{2,1,0:T(8,128)(2,1)}, bf16[4,288,3072]{2,1,0:T(8,128)(2,1)}, bf16[4,288,768]{2,1,0:T(8,128)(2,1)}, bf16[4,288,2304]{2,1,0:T(8,128...) custom-call(f32[8,128]{1,0:T(8,128)} %get-tuple-element.77.shares, ...), custom_call_target="tpu_custom_call" | custom-call | tf_op jit(solution)/shard_map/backward/pallas_call | solution.py:494
  418.9 0.8 slice.52
  419.8 4.5 bitcast_convert_fusion.3
  424.3 7.9 %bitcast_convert_fusion.1 = bf16[768,3072]{1,0:T(8,128)(2,1)} fusion(bf16[4,288,768]{2,1,0:T(8,128)(2,1)S(1)} %copy-done.12, bf16[4,288,3072]{2,1,0:T(8,128)(2,1)S(1)} %copy-done.7), kind=kOutput, calls=%fused_computation.1 | convolution fusion | flops 5438177280 | bytes 13565952 | tf_op jit(solution)/shard_map/dot_general | solution.py:38
  432.7 1.2 fusion.4
  433.9 1.2 fusion.7.refs_8_
  436.2 6.3 %bitcast_convert_fusion.2 = bf16[768,2304]{1,0:T(8,128)(2,1)} fusion(bf16[4,288,768]{2,1,0:T(8,128)(2,1)S(1)} %copy-done.10, bf16[4,288,2304]{2,1,0:T(8,128)(2,1)S(1)} %copy-done.8), kind=kOutput, calls=%fused_computation.2 | convolution fusion | flops 4078632960 | bytes 10616832 | tf_op jit(solution)/shard_map/dot_general | solution.py:38
  442.5 8.0 %bitcast_convert_fusion = bf16[768,3072]{1,0:T(8,128)(2,1)} fusion(bf16[4,288,768]{2,1,0:T(8,128)(2,1)S(1)} %copy-done.9, bf16[4,288,3072]{2,1,0:T(8,128)(2,1)S(1)} %bitcast.55), kind=kOutput, calls=%fused_computation | convolution fusion | flops 5438177280 | bytes 13565952 | tf_op jit(solution)/shard_map/dot_general | solution.py:38
  450.5 128.0 %deliver.1 = (bf16[8,288,384]{2,1,0:T(8,128)(2,1)}, bf16[12,288,384]{2,1,0:T(8,128)(2,1)}, bf16[288,384]{1,0:T(8,128)(2,1)}, f32[16,384]{1,0:T(8,128)}, f32[48,1...) custom-call(s32[12]{0:T(128)} %get-tuple-element.118.refs_0_, ...), custom_call_target="tpu_custom_call" | custom-call | tf_op jit(solution)/shard_map/deliver/pallas_call | solution.py:685
  578.5 0.7 slice.63
  579.2 1.6 slice_reduce_fusion.1
  581.5 1.3 slice_bitcast_fusion
  582.8 1.4 slice.54
  584.2 1.6 fusion.16
  585.8 9.9 %place_docs.1 = f32[16,288,384]{2,1,0:T(8,128)} custom-call(s32[12]{0:T(128)} %slice_reduce_fusion.want, bf16[12,288,384]{2,1,0:T(8,128)(2,1)} %get-tuple-element.102.arrived), custom_call_target="tpu_custom_call" | custom-call | tf_op jit(solution)/shard_map/place_docs/pallas_call | solution.py:710
  595.7 0.7 copy.68
  596.4 1.2 copy.69
  598.8 0.7 copy.72
  599.5 0.7 copy.73
  (53 shorter events, 9.9 us)
Async XLA Ops:
  352.5 67.2 %copy-start.6 = (f32[8,128]{1,0:T(8,128)S(1)}, f32[8,128]{1,0:T(8,128)}, u32[]{:S(2)}) copy-start(f32[8,128]{1,0:T(8,128)} %get-tuple-element.78.dsum) | copy-start | bytes 12292
  352.5 67.2 %copy-start.11 = (bf16[4,288,768]{2,1,0:T(8,128)(2,1)S(1)}, bf16[4,288,768]{2,1,0:T(8,128)(2,1)}, u32[]{:S(2)}) copy-start(bf16[4,288,768]{2,1,0:T(8,128)(2,1)} %get-tuple-element.95) | copy-start | bytes 5308420
  419.8 4.5 copy-start.7
  419.8 4.5 copy-start.12
  424.3 8.4 %copy-start = (bf16[4,288,768]{2,1,0:T(8,128)(2,1)S(1)}, bf16[4,288,768]{2,1,0:T(8,128)(2,1)}, u32[]{:S(2)}) copy-start(bf16[4,288,768]{2,1,0:T(8,128)(2,1)} %get-tuple-element.89.refs_3_) | copy-start | bytes 5308420
  432.7 2.9 copy-start.8
  432.7 3.5 copy-start.10
  433.9 8.6 %slice-start = ((s8[7077888]{0:T(1024)(128)(4,1)}), s8[4194304]{0:T(1024)(128)(4,1)S(1)}, s32[]{:S(2)}) async-start(s8[7077888]{0:T(1024)(128)(4,1)} %bitcast.54), calls=%async_computation | async-start | bytes 8388608
  436.2 6.3 %slice-start.1 = ((s8[7077888]{0:T(1024)(128)(4,1)}), s8[2883584]{0:T(1024)(128)(4,1)S(1)}, s32[]{:S(2)}) async-start(s8[7077888]{0:T(1024)(128)(4,1)} %bitcast.54), calls=%async_computation.1 | async-start | bytes 5767168
  436.2 6.3 %copy-start.9 = (bf16[4,288,768]{2,1,0:T(8,128)(2,1)S(1)}, bf16[4,288,768]{2,1,0:T(8,128)(2,1)}, u32[]{:S(2)}) copy-start(bf16[4,288,768]{2,1,0:T(8,128)(2,1)} %get-tuple-element.92) | copy-start | bytes 5308420
  585.8 9.9 %copy-start.4 = (bf16[288,384]{1,0:T(8,128)(2,1)S(1)}, bf16[288,384]{1,0:T(8,128)(2,1)}, u32[]{:S(2)}) copy-start(bf16[288,384]{1,0:T(8,128)(2,1)} %get-tuple-element.98) | copy-start | bytes 663556
  585.8 10.6 %copy-start.1 = (bf16[8,288,384]{2,1,0:T(8,128)(2,1)S(1)}, bf16[8,288,384]{2,1,0:T(8,128)(2,1)}, u32[]{:S(2)}) copy-start(bf16[8,288,384]{2,1,0:T(8,128)(2,1)} %get-tuple-element.148) | copy-start | bytes 5308420
  596.4 1.2 copy-start.13
  596.4 1.7 copy-start.5
  596.4 2.4 copy-start.3
  596.4 3.1 copy-start.2
